TPU v7x, 256 devices: a whole 4x4x8 slice. The times are simulated.
256 devices in a mesh: seq: 16 (over x, y), mp: 16 (over z, core).
Axes of the slice: x: 4, y: 4, z: 8, core: 2. Of those that a mesh axis runs over, the one named last changes fastest.
Arguments:
- hidden: bfloat16 [12288, 4096], P('seq', 'mp'), may hold values from -40 to 40
- encodings: bfloat16 [512, 256, 896], P('seq', 'mp'), may hold values from -32 to 32
- span_owner: int32 [192, 1], replicated, may hold values from 0 to 15; in each aligned block of 12 rows (0 to 11, 12 to 23, ...) at most 2 rows name the same one
- w_query: bfloat16 [4096, 4096], P(None, 'mp'), may hold values from -2 to 2
- w_key: bfloat16 [896, 4096], P(None, 'mp'), may hold values from -2 to 2
- w_value: bfloat16 [896, 4096], P(None, 'mp'), may hold values from -0.1875 to 0.1875
- w_out: bfloat16 [4096, 4096], P('mp'), may hold values from -0.5 to 0.5
- cotangent: bfloat16 [12288, 4096], P('seq', 'mp'), may hold values from -6 to 6
Outputs:
- branch: bfloat16 [12288, 4096], P('seq', 'mp')
- grad_hidden: bfloat16 [12288, 4096], P('seq', 'mp')
- grad_encodings: bfloat16 [512, 256, 896], P('seq', 'mp')
Inputs may be any that keep to these rules, and one draw needn't show every extreme that they name: `span_owner`: in each decoder shard's 12 spans (aligned blocks of rows) no encoder shard is named more than 2 times, and in every draw some shard of some block is named exactly 2 times.
All inputs are finite; a program needn't handle non-finite values.
Results may differ from a plain program's by a relative error of at most 0.025.
Values may be sent and summed in bfloat16 or wider, within the bound.
No kernel may reach another device: no remote copies, remote signals or barrier semaphores. Data moves between devices by JAX's collectives and lax.ppermute only.
A program may use at most 128 MiB of HBM per device.

v0:
```python
import jax
import jax.numpy as jnp
from jax import lax
from jax.sharding import PartitionSpec as P

DH = 128
SPAN = 64


def from_behind(value, axis, steps):
    count = lax.axis_size(axis)
    initial, last = (max(0, -steps), min(count, count - steps))
    return lax.ppermute(value, axis, [(source, source + steps) for source in range(initial, last)])


def attend(query_sets, key_sets, value_sets):
    scores = jnp.einsum(
        "sqhe,srhe->shqr", query_sets, key_sets, preferred_element_type=jnp.float32
    ) * DH ** (-0.5)
    highest = jnp.max(scores, axis=-1, keepdims=True)
    raised = jnp.exp(scores - highest)
    weights = raised / jnp.sum(raised, axis=-1, keepdims=True)
    weights_low = weights.astype(jnp.bfloat16)
    attended = jnp.einsum(
        "shqr,srhe->sqhe", weights_low, value_sets, preferred_element_type=jnp.float32
    ).astype(jnp.bfloat16)
    return (weights, weights_low, attended)


def attend_back(query_sets, key_sets, value_sets, weights, weights_low, grad_sets):
    grad_weights = jnp.einsum(
        "sqhe,srhe->shqr", grad_sets, value_sets, preferred_element_type=jnp.float32
    )
    inner_sum = jnp.sum(weights * grad_weights, axis=-1, keepdims=True)
    grad_scores = (weights * (grad_weights - inner_sum) * DH ** (-0.5)).astype(jnp.bfloat16)
    grad_queries = jnp.einsum(
        "shqr,srhe->sqhe", grad_scores, key_sets, preferred_element_type=jnp.float32
    )
    grad_keys = jnp.einsum(
        "shqr,sqhe->srhe", grad_scores, query_sets, preferred_element_type=jnp.float32
    )
    grad_values = jnp.einsum(
        "shqr,sqhe->srhe", weights_low, grad_sets, preferred_element_type=jnp.float32
    )
    return (grad_queries, grad_keys, grad_values)


def split_pairs(span_sets, columns):
    set_count = span_sets.shape[0]
    row_count = span_sets.shape[1]
    key_sets = span_sets[:, :, :columns].reshape(set_count, row_count, columns // DH, DH)
    value_sets = span_sets[:, :, columns:].reshape(set_count, row_count, columns // DH, DH)
    return (key_sets, value_sets)


def join_grads(grad_k_sets, grad_v_sets, columns):
    set_count = grad_k_sets.shape[0]
    row_count = grad_k_sets.shape[1]
    return jnp.concatenate(
        [
            grad_k_sets.reshape(set_count, row_count, columns),
            grad_v_sets.reshape(set_count, row_count, columns),
        ],
        axis=2,
    )


def on_device(hidden, encodings, span_owner, w_query, w_key, w_value, w_out, cotangent):
    seq_count = lax.axis_size("seq")
    shard_index = lax.axis_index("seq")
    capacity = encodings.shape[0] // seq_count
    token_count = hidden.shape[0]
    span_count = token_count // SPAN
    columns = w_query.shape[1]
    groups = columns // DH
    leading = SPAN - 1
    owners = lax.dynamic_slice_in_dim(span_owner[:, 0], shard_index * span_count, span_count)
    positions = jnp.arange(span_count, dtype=jnp.int32)
    earlier = (owners[:, None] == owners[None, :]) & (positions[None, :] < positions[:, None])
    picked = owners * capacity + jnp.sum(earlier.astype(jnp.int32), axis=1)
    both_weights = jnp.concatenate([w_key, w_value], axis=1)
    queries = jnp.dot(
        lax.all_gather(hidden, "mp", axis=1, tiled=True),
        w_query,
        preferred_element_type=jnp.float32,
    ).astype(jnp.bfloat16)
    grad_attended = lax.dot_general(
        lax.all_gather(cotangent, "mp", axis=1, tiled=True),
        w_out,
        (((1,), (1,)), ((), ())),
        preferred_element_type=jnp.float32,
    ).astype(jnp.bfloat16)
    received = lax.all_to_all(encodings, "seq", split_axis=0, concat_axis=0, tiled=True)
    every_row = lax.all_gather(received, "mp", axis=1, tiled=True)
    shard_part = jnp.take(every_row, picked, axis=0)
    flattened = shard_part.reshape(-1, shard_part.shape[2])
    projected = jnp.dot(flattened, both_weights, preferred_element_type=jnp.float32).astype(
        jnp.bfloat16
    )
    key_values = projected.reshape(shard_part.shape[0], shard_part.shape[1], 2 * columns)
    previous = from_behind(key_values[span_count - 1], "seq", 1)
    key_sets, value_sets = split_pairs(
        jnp.concatenate([previous[None], key_values], axis=0), columns
    )
    pad_front = jnp.zeros((1, columns), jnp.bfloat16)
    pad_back = jnp.zeros((leading, columns), jnp.bfloat16)
    query_sets = jnp.concatenate([pad_front, queries, pad_back], axis=0).reshape(
        span_count + 1, SPAN, groups, DH
    )
    grad_sets = jnp.concatenate([pad_front, grad_attended, pad_back], axis=0).reshape(
        span_count + 1, SPAN, groups, DH
    )
    weights, weights_low, attended_sets = attend(query_sets, key_sets, value_sets)
    attended = attended_sets.reshape(-1, columns)[1 : token_count + 1]
    grad_q_sets, grad_k_sets, grad_v_sets = attend_back(
        query_sets, key_sets, value_sets, weights, weights_low, grad_sets
    )
    grad_queries = grad_q_sets.reshape(-1, columns)[1 : token_count + 1].astype(jnp.bfloat16)
    grad_pairs = join_grads(grad_k_sets, grad_v_sets, columns)
    returned = from_behind(grad_pairs[0].astype(jnp.bfloat16), "seq", -1).astype(jnp.float32)
    grad_key_values = grad_pairs[1:].at[span_count - 1].add(returned)
    branch_terms = jnp.dot(attended, w_out, preferred_element_type=jnp.float32)
    branch = lax.psum_scatter(
        branch_terms.astype(jnp.bfloat16), "mp", scatter_dimension=1, tiled=True
    )
    hidden_terms = lax.dot_general(
        grad_queries, w_query, (((1,), (1,)), ((), ())), preferred_element_type=jnp.float32
    )
    grad_hidden = lax.psum_scatter(
        hidden_terms.astype(jnp.bfloat16), "mp", scatter_dimension=1, tiled=True
    )
    grad_low = grad_key_values.astype(jnp.bfloat16)
    shares = lax.psum_scatter(
        jnp.einsum(
            "crk,dk->rcd", grad_low, both_weights, preferred_element_type=jnp.float32
        ).astype(jnp.bfloat16),
        "mp",
        scatter_dimension=0,
        tiled=True,
    )
    outgoing = (
        jnp.zeros(encodings.shape, jnp.bfloat16).at[picked].set(jnp.transpose(shares, (1, 0, 2)))
    )
    grad_encodings = lax.all_to_all(outgoing, "seq", split_axis=0, concat_axis=0, tiled=True)
    return (branch, grad_hidden, grad_encodings)


def solution(mesh):
    return jax.shard_map(
        on_device,
        mesh=mesh,
        in_specs=(
            P("seq", "mp"),
            P("seq", "mp", None),
            P(),
            P(None, "mp"),
            P(None, "mp"),
            P(None, "mp"),
            P("mp", None),
            P("seq", "mp"),
        ),
        out_specs=(P("seq", "mp"), P("seq", "mp"), P("seq", "mp", None)),
        check_vma=False,
    )
```

profile of v0, /device:TPU:2, one launch (start us, length us, event | category | flops | bytes accessed | tf_op | source)
XLA Modules:
  0.0 503.8 jit_solution(15946810754894400640)
XLA Ops:
  7.2 0.0 all-gather.8.cloned.1.call-start
  7.2 0.7 all-gather.8.cloned.1.call-update
  7.9 0.0 all-gather.4.cloned.1.call-start
  8.0 21.3 %all_to_all.10 = bf16[32,16,896]{2,1,0:T(8,128)(2,1)} all-to-all(bf16[32,16,896]{2,1,0:T(8,128)(2,1)} %param.11), channel_id=1, replica_groups=mesh['seq'=16,'mp'=16] {'seq'}, dimensions={0} | all-to-all | bytes 1835008 | tf_op jit(solution)/shard_map/all_to_all | solution.py:93
  29.3 0.0 all-gather.6.cloned.1.call-start
  29.4 0.7 all-gather.6.cloned.1.call-update
  30.1 0.0 reduce-scatter.8.cloned.1.call-start
  30.1 0.1 fusion.46
  30.2 0.2 convert_reduce_fusion
  30.4 0.1 and_bitcast_fusion
  30.5 0.1 broadcast_in_dim.34
  30.6 0.1 pad.9.clone
  30.7 0.8 constant_dynamic-update-slice_fusion.1
  31.5 0.8 constant_dynamic-update-slice_fusion
  32.3 36.9 %all-gather.8.cloned.1.call-done = bf16[768,4096]{1,0:T(8,128)(2,1)} async-done(((bf16[768,256]{1,0:T(8,128)(2,1)}), bf16[768,4096]{1,0:T(8,128)(2,1)}) %all-gather.8.cloned.1.call-update) | async-done | bytes 6291472 | tf_op jit(solution)/shard_map/all_gather | solution.py:88
  69.2 4.6 convolution_convert_fusion.4
  73.8 81.0 %all-gather.4.cloned.1.call-done = bf16[32,256,896]{2,1,0:T(8,128)(2,1)} async-done(((bf16[32,16,896]{2,1,0:T(8,128)(2,1)}), bf16[32,256,896]{2,1,0:T(8,128)(2,1)}) %all-gather.4.cloned.1.call-update) | async-done | bytes 14680080 | tf_op jit(solution)/shard_map/all_gather | solution.py:94
  154.8 9.1 %gather_fusion = bf16[12,256,896]{2,1,0:T(8,128)(2,1)} fusion(bf16[32,256,896]{2,1,0:T(8,128)(2,1)} %all-gather.4.cloned.1.call-done, s32[1024]{0:T(1024)S(1)} %pad_clamp_fusion), kind=kCustom, calls=%fused_computation | custom fusion | bytes 11010096 | tf_op jit(solution)/shard_map/jit(_take)/gather | solution.py:95
  163.9 3.8 bitcast_select_fusion
  167.7 4.8 convolution_convert_fusion.2
  172.6 1.6 copy-done.6
  174.2 0.7 slice.57
  174.9 3.6 collective-permute-start
  178.5 33.0 %all-gather.6.cloned.1.call-done = bf16[768,4096]{1,0:T(8,128)(2,1)} async-done(((bf16[768,256]{1,0:T(8,128)(2,1)}), bf16[768,4096]{1,0:T(8,128)(2,1)}) %all-gather.6.cloned.1.call-update) | async-done | bytes 6291472 | tf_op jit(solution)/shard_map/all_gather | solution.py:83
  211.5 5.2 %convolution_convert_fusion.5 = bf16[768,256]{1,0:T(8,128)(2,1)S(1)} fusion(bf16[768,4096]{1,0:T(8,128)(2,1)} %all-gather.6.cloned.1.call-done, bf16[4096,256]{1,0:T(8,128)(2,1)} %param.13), kind=kOutput, calls=%fused_computation.32 | convolution fusion | flops 1610809344 | bytes 8781824 | tf_op jit(solution)/shard_map/dot_general | solution.py:82
  216.7 0.4 maximum_maximum_fusion.1
  217.1 0.1 reshape.88
  217.2 0.1 reshape.91
  217.3 4.7 copy.50
  222.0 1.1 copy.49
  223.1 2.2 pad_maximum_fusion
  225.3 0.4 fusion.40
  225.7 0.8 copy-done.4
  226.5 1.8 exponential_reduce_fusion
  228.3 1.6 fusion.37
  229.9 6.4 %fusion.31 = f32[13,2,128,256]{3,2,1,0:T(8,128)} fusion(bf16[13,64,2,128]{3,2,1,0:T(2,128)(2,1)S(1)} %reshape.91, f32[13,2,64]{2,1,0:T(2,128)S(1)} %get-tuple-element.21, f32[13,2,64,256]{3,2,1,0:T(8,128)} %copy-done.3), kind=kOutput, calls=%fused_computation.48 | convolution fusion | flops 110757760 | bytes 5544448 | tf_op jit(solution)/shard_map/shqr,sqhe->srhe/dot_general | solution.py:42
  236.3 14.3 %fusion.11 = f32[13,2,128,256]{3,2,1,0:T(8,128)} fusion(f32[13,2,64,256]{3,2,1,0:T(8,128)} %fusion.37, bf16[13,64,2,128]{3,2,1,0:T(2,128)(2,1)S(1)} %reshape.88, f32[13,2,64,256]{3,2,1,0:T(8,128)} %get-tuple-element.22, f32[13,2,64]{2,1,0:T(2,128)S(1)} %get-tuple-element.21), kind=kOutput, calls=%fused_computation.27 | convolution fusion | flops 112035712 | bytes 7248384 | tf_op jit(solution)/shard_map/shqr,sqhe->srhe/dot_general | solution.py:39
  250.6 4.7 copy.61
  255.3 4.7 copy.62
  260.1 1.2 fusion.42
  261.3 5.1 %collective-permute-start.1 = (bf16[256,512]{1,0:T(8,128)(2,1)S(1)}, bf16[256,512]{1,0:T(8,128)(2,1)S(1)}, u32[]{:S(2)}, u32[]{:S(2)}) collective-permute-start(bf16[256,512]{1,0:T(8,128)(2,1)S(1)} %fusion.42), channel_id=1, source_target_pairs={{16,0},{32,16},{48,32},{64,48},{80,64},{96,80},{112,96},{128,112},... | collective-permute-start | bytes 786440 | tf_op jit(solution)/shard_map/ppermute | solution.py:13
  266.4 0.4 fusion.2
  266.9 5.3 %collective-permute-done.1 = bf16[256,512]{1,0:T(8,128)(2,1)S(1)} collective-permute-done((bf16[256,512]{1,0:T(8,128)(2,1)S(1)}, bf16[256,512]{1,0:T(8,128)(2,1)S(1)}, u32[]{:S(2)}, u32[]{:S(2)}) %collective-permute-start.1) | collective-permute-done | bytes 262176 | tf_op jit(solution)/shard_map/ppermute | solution.py:13
  272.2 0.1 fusion.29
  272.2 6.0 %convert_bitcast_fusion = bf16[256,12,896]{0,2,1:T(8,128)(2,1)} fusion(bf16[12,256,512]{2,1,0:T(8,128)(2,1)S(1)} %fusion.29, bf16[896,512]{1,0:T(8,128)(2,1)} %constant_dynamic-update-slice_fusion), kind=kOutput, calls=%fused_computation.12 | convolution fusion | flops 2821324800 | bytes 9568256 | tf_op jit(solution)/shard_map/crk,dk->rcd/dot_general | solution.py:134
  278.2 11.4 %copy.63 = bf16[256,12,896]{2,1,0:T(8,128)(2,1)} copy(bf16[256,12,896]{0,2,1:T(8,128)(2,1)} %convert_bitcast_fusion) | data formatting | bytes 11010048 | tf_op jit(solution)/shard_map/convert_element_type | solution.py:136
  289.6 0.0 reduce-scatter.4.cloned.1.call-start
  289.7 4.9 fusion.22
  294.6 0.5 copy.54
  295.1 0.1 copy.82
  295.2 4.5 convolution_convert_fusion.1
  299.7 0.0 reduce-scatter.6.cloned.1.call-start
  299.7 12.9 %fusion.19 = bf16[13,64,2,128]{3,1,2,0:T(8,128)(2,1)S(1)} fusion(bf16[13,256,2,128]{1,3,2,0:T(8,128)(2,1)} %bitcast.62, f32[13,2,64,256]{3,2,1,0:T(8,128)} %fusion.37, f32[13,2,64,256]{3,2,1,0:T(8,128)} %get-tuple-element.22, f32[13,2,64]{2,1,0:T(2,128)S(1)} %get-tuple-element.21), kind=kOutput, calls=%fused_computation.33 | convolution fusion | flops 112248704 | bytes 5544448 | tf_op jit(solution)/shard_map/shqr,srhe->sqhe/dot_general | solution.py:36
  312.6 0.5 copy.58
  313.1 0.1 copy.81
  313.1 6.1 %convolution_convert_fusion = bf16[768,4096]{1,0:T(8,128)(2,1)} fusion(bf16[4096,256]{1,0:T(8,128)(2,1)} %param.13, bf16[832,256]{1,0:T(8,128)(2,1)S(1)} %bitcast.69), kind=kOutput, calls=%fused_computation.8 | convolution fusion | flops 1613758464 | bytes 8781824 | tf_op jit(solution)/shard_map/dot_general | solution.py:126
  319.2 39.1 %reduce-scatter.8.cloned.1.call-done = bf16[16,12,896]{2,1,0:T(8,128)(2,1)} async-done(((bf16[256,12,896]{2,1,0:T(8,128)(2,1)}), bf16[16,12,896]{2,1,0:T(8,128)(2,1)}) %reduce-scatter.8.cloned.1.call-update) | async-done | bytes 344080 | tf_op jit(solution)/shard_map/reduce_scatter | solution.py:133
  358.3 1.1 copy.64
  359.4 0.1 broadcast_in_dim.41
  359.5 1.0 scatter_fusion
  360.5 17.9 %all_to_all.11 = bf16[32,16,896]{2,1,0:T(8,128)(2,1)} all-to-all(bf16[32,16,896]{2,1,0:T(8,128)(2,1)S(1)} %scatter_fusion), channel_id=1, replica_groups=mesh['seq'=16,'mp'=16] {'seq'}, dimensions={0} | all-to-all | bytes 1835008 | tf_op jit(solution)/shard_map/all_to_all | solution.py:144
  378.4 48.6 %reduce-scatter.4.cloned.1.call-done = bf16[768,256]{1,0:T(8,128)(2,1)} async-done(((bf16[768,4096]{1,0:T(8,128)(2,1)}), bf16[768,256]{1,0:T(8,128)(2,1)}) %reduce-scatter.4.cloned.1.call-update) | async-done | bytes 393232 | tf_op jit(solution)/shard_map/reduce_scatter | solution.py:123
  426.9 67.9 %reduce-scatter.6.cloned.1.call-done = bf16[768,256]{1,0:T(8,128)(2,1)} async-done(((bf16[768,4096]{1,0:T(8,128)(2,1)}), bf16[768,256]{1,0:T(8,128)(2,1)}) %reduce-scatter.6.cloned.1.call-update) | async-done | bytes 393232 | tf_op jit(solution)/shard_map/reduce_scatter | solution.py:129
  494.8 2.2 copy.87
  (27 shorter events, 0.1 us)
Async XLA Ops:
  7.2 62.0 %copy-start = (bf16[256,4096]{1,0:T(8,128)(2,1)S(1)}, bf16[256,4096]{1,0:T(8,128)(2,1)}, u32[]{:S(2)}) copy-start(bf16[256,4096]{1,0:T(8,128)(2,1)} %param.16) | copy-start | bytes 6291460
  7.2 22.9 %copy-start.9 = (s32[192,1]{0,1:T(1,128)S(1)}, s32[192,1]{0,1:T(1,128)}, u32[]{:S(2)}) copy-start(s32[192,1]{0,1:T(1,128)} %param.12) | copy-start | bytes 2308
  7.2 23.5 %copy-start.7 = (bf16[896,256]{1,0:T(8,128)(2,1)S(1)}, bf16[896,256]{1,0:T(8,128)(2,1)}, u32[]{:S(2)}) copy-start(bf16[896,256]{1,0:T(8,128)(2,1)} %param.14) | copy-start | bytes 1376260
  7.2 62.0 %all-gather.8.cloned.1.call-start = ((), (), s32[]{:S(2)}) async-start(), calls=%async_computation.8 | async-start | bytes 6684672 | tf_op jit(solution)/shard_map/all_gather | solution.py:88
  7.9 23.6 %copy-start.8 = (bf16[896,256]{1,0:T(8,128)(2,1)S(1)}, bf16[896,256]{1,0:T(8,128)(2,1)}, u32[]{:S(2)}) copy-start(bf16[896,256]{1,0:T(8,128)(2,1)} %param.15) | copy-start | bytes 1376260
  7.9 146.8 %all-gather.4.cloned.1.call-start = ((), (), s32[]{:S(2)}) async-start(), calls=%async_computation.5 | async-start | bytes 15597568 | tf_op jit(solution)/shard_map/all_gather | solution.py:94
  29.3 182.2 %all-gather.6.cloned.1.call-start = ((), (), s32[]{:S(2)}) async-start(), calls=%async_computation.6 | async-start | bytes 6684672 | tf_op jit(solution)/shard_map/all_gather | solution.py:83
  30.1 328.2 %reduce-scatter.8.cloned.1.call-start = ((), (), s32[]{:S(2)}) async-start(), calls=%async_computation.10 | async-start | bytes 7798784 | tf_op jit(solution)/shard_map/reduce_scatter | solution.py:133
  172.6 1.7 copy-start.6
  174.9 47.1 %collective-permute-start = (bf16[256,512]{1,0:T(8,128)(2,1)}, bf16[256,512]{1,0:T(8,128)(2,1)}, u32[]{:S(2)}, u32[]{:S(2)}) collective-permute-start(bf16[256,512]{1,0:T(8,128)(2,1)} %slice.57), channel_id=1, source_target_pairs={{0,16},{16,32},{32,48},{48,64},{64,80},{80,96},{96,112},{112,128},... | collective-permute-start | bytes 786440 | tf_op jit(solution)/shard_map/ppermute | solution.py:13
  225.3 1.2 copy-start.4
  225.3 2.9 copy-start.5
  226.5 1.8 copy-start.3
  260.1 6.4 %copy-start.1 = (f32[13,256,256]{2,1,0:T(8,128)S(1)}, f32[13,256,256]{2,1,0:T(8,128)}, u32[]{:S(2)}) copy-start(f32[13,256,256]{2,1,0:T(8,128)} %copy.61) | copy-start | bytes 10223620
  260.1 6.4 %copy-start.2 = (f32[13,256,256]{2,1,0:T(8,128)S(1)}, f32[13,256,256]{2,1,0:T(8,128)}, u32[]{:S(2)}) copy-start(f32[13,256,256]{2,1,0:T(8,128)} %copy.62) | copy-start | bytes 10223620
  261.3 10.9 %collective-permute-start.1 = (bf16[256,512]{1,0:T(8,128)(2,1)S(1)}, bf16[256,512]{1,0:T(8,128)(2,1)S(1)}, u32[]{:S(2)}, u32[]{:S(2)}) collective-permute-start(bf16[256,512]{1,0:T(8,128)(2,1)S(1)} %fusion.42), channel_id=1, source_target_pairs={{16,0},{32,16},{48,32},{64,48},{80,64},{96,80},{112,96},{128,112},... | collective-permute-start | bytes 786440 | tf_op jit(solution)/shard_map/ppermute | solution.py:13
  289.6 137.3 %reduce-scatter.4.cloned.1.call-start = ((), (), s32[]{:S(2)}) async-start(), calls=%async_computation.7 | async-start | bytes 6684672 | tf_op jit(solution)/shard_map/reduce_scatter | solution.py:123
  299.7 195.1 %reduce-scatter.6.cloned.1.call-start = ((), (), s32[]{:S(2)}) async-start(), calls=%async_computation.9 | async-start | bytes 6684672 | tf_op jit(solution)/shard_map/reduce_scatter | solution.py:129
Sparse Core Ops, SparseCore 0:
  9.8 59.3 all-gather.7
  71.0 83.7 all-gather.3
  156.6 54.9 all-gather.5
  289.8 68.5 reduce-scatter.7
  361.3 65.5 reduce-scatter.3
  429.9 64.8 reduce-scatter.5
where the time goes:
time: 505 us; the launch traced here: 504 us
  waiting for transfers between devices  313 us (62%)
  matrix products  71.7 us (14%)
  local copies, waits for them, and re-layouts  46.3 us (9%)
  blocking collectives  39.2 us (8%)
  between operations  14.4 us (3%)
  other arithmetic  10.1 us (2%)
  starting transfers between devices  8.93 us (2%)
    all_gather x1, waiting for transfers between devices, on_device(): every_row = lax.all_gather(received, 'mp', axis=1, tiled=True)  81 us
    reduce_scatter x1, waiting for transfers between devices, on_device(): lax.psum_scatter(hidden_terms.astype(jnp.bfloat16), 'mp', scatter_dimensi...  67.9 us
    reduce_scatter x1, waiting for transfers between devices, on_device(): lax.psum_scatter(branch_terms.astype(jnp.bfloat16), 'mp', scatter_dimensi...  48.6 us
    reduce_scatter x1, waiting for transfers between devices, on_device(): lax.psum_scatter(jnp.einsum('crk,dk->rcd', grad_low, both_weights, prefer...  39.1 us
    all_gather x1, waiting for transfers between devices, on_device(): lax.all_gather(cotangent, 'mp', axis=1, tiled=True)  36.9 us
    all_gather x1, waiting for transfers between devices, on_device(): lax.all_gather(hidden, 'mp', axis=1, tiled=True)  33 us
    all_to_all x1, blocking collectives, on_device(): lax.all_to_all(encodings, 'seq', split_axis=0, concat_axis=0, tiled=True)  21.3 us
    all_to_all x1, blocking collectives, on_device(): lax.all_to_all(outgoing, 'seq', split_axis=0, concat_axis=0, tiled=True)  17.9 us
  transfers between devices with their start and end apart: 8, of which 7 were waited for; matrix products, arithmetic and copies ran while one was open for 13% of the time, Pallas kernels for 0%

commit v1 on v0

--- a/solution.py
+++ b/solution.py
@@ -5,6 +5,13 @@
 
 DH = 128
 SPAN = 64
+
+
+def gather_over(array, mesh_axis, along):
+    peers = lax.axis_size(mesh_axis)
+    blocks = jnp.stack([array for _ in range(peers)])
+    blocks = lax.all_to_all(blocks, mesh_axis, split_axis=0, concat_axis=0)
+    return jnp.concatenate(blocks, axis=along)
 
 
 def from_behind(value, axis, steps):
@@ -85,7 +92,7 @@
         preferred_element_type=jnp.float32,
     ).astype(jnp.bfloat16)
     grad_attended = lax.dot_general(
-        lax.all_gather(cotangent, "mp", axis=1, tiled=True),
+        gather_over(cotangent, "mp", 1),
         w_out,
         (((1,), (1,)), ((), ())),
         preferred_element_type=jnp.float32,

time: 505 us -> 599 us (1.19)
  waiting for transfers between devices: 313 us -> 396 us
  starting transfers between devices: 8.93 us -> 16.8 us
    all_to_all x0 -> x1, waiting for transfers between devices: none -> 197 us  [gather_over(): blocks = lax.all_to_all(blocks, mesh_axis, split_axis=0, concat_axis=0)]
    all_gather x1, waiting for transfers between devices: 81 us -> 4.95 us  [on_device(): every_row = lax.all_gather(received, 'mp', axis=1, tiled=True)]
    all_gather x1 -> x0, waiting for transfers between devices: 36.9 us -> none  [on_device(): lax.all_gather(cotangent, 'mp', axis=1, tiled=True)]
    all_to_all x0 -> x1, starting transfers between devices: none -> 8.75 us  [gather_over(): blocks = lax.all_to_all(blocks, mesh_axis, split_axis=0, concat_axis=0)]
  transfers between devices with their start and end apart: 8 -> 8, of which waited for: 7 -> 7; matrix products, arithmetic and copies ran while one was open for 13% -> 12% of each run, Pallas kernels for 0% -> 0%
where the time goes in v1:
time: 599 us; the launch traced here: 598 us
  waiting for transfers between devices  396 us (66%)
  matrix products  71.8 us (12%)
  local copies, waits for them, and re-layouts  49.7 us (8%)
  blocking collectives  39 us (7%)
  starting transfers between devices  16.8 us (3%)
  between operations  14.1 us (2%)
  other arithmetic  10 us (2%)
    all_to_all x1, waiting for transfers between devices, gather_over(): blocks = lax.all_to_all(blocks, mesh_axis, split_axis=0, concat_axis=0)  197 us
    reduce_scatter x1, waiting for transfers between devices, on_device(): lax.psum_scatter(hidden_terms.astype(jnp.bfloat16), 'mp', scatter_dimensi...  67.9 us
    reduce_scatter x1, waiting for transfers between devices, on_device(): lax.psum_scatter(branch_terms.astype(jnp.bfloat16), 'mp', scatter_dimensi...  48.5 us
    reduce_scatter x1, waiting for transfers between devices, on_device(): lax.psum_scatter(jnp.einsum('crk,dk->rcd', grad_low, both_weights, prefer...  39.1 us
    all_gather x1, waiting for transfers between devices, on_device(): lax.all_gather(hidden, 'mp', axis=1, tiled=True)  32.9 us
    all_to_all x1, blocking collectives, on_device(): lax.all_to_all(encodings, 'seq', split_axis=0, concat_axis=0, tiled=True)  21.3 us
    all_to_all x1, blocking collectives, on_device(): lax.all_to_all(outgoing, 'seq', split_axis=0, concat_axis=0, tiled=True)  17.7 us
    dot_general x1, matrix products, attend_back(): jnp.einsum('shqr,sqhe->srhe', grad_scores, query_sets, preferred_element_...  14.3 us
  transfers between devices with their start and end apart: 8, of which 7 were waited for; matrix products, arithmetic and copies ran while one was open for 12% of the time, Pallas kernels for 0%

profile of v1, /device:TPU:2, one launch (start us, length us, event | category | flops | bytes accessed | tf_op | source)
XLA Modules:
  0.0 597.8 jit_solution(12023099582701534982)
XLA Ops:
  7.2 21.3 %all_to_all.15 = bf16[32,16,896]{2,1,0:T(8,128)(2,1)} all-to-all(bf16[32,16,896]{2,1,0:T(8,128)(2,1)} %param.11), channel_id=1, replica_groups=mesh['seq'=16,'mp'=16] {'seq'}, dimensions={0} | all-to-all | bytes 1835008 | tf_op jit(solution)/shard_map/all_to_all | solution.py:100
  28.6 0.2 copy.57
  28.8 3.2 stack.2
  32.0 8.7 %all-to-all-start.1 = ((bf16[16,768,256]{1,2,0:T(8,128)(2,1)}), bf16[16,768,256]{1,2,0:T(8,128)(2,1)}, u32[]{:S(2)}, u32[]{:S(2)}) async-start(bf16[16,768,256]{1,2,0:T(8,128)(2,1)} %stack.2), calls=%async_computation.2 | async-start | bytes 12582912 | tf_op jit(solution)/shard_map/all_to_all | solution.py:13
  40.7 0.0 all-gather.5.cloned.1.call-start
  40.8 0.7 all-gather.5.cloned.1.call-update
  41.5 0.0 reduce-scatter.8.cloned.1.call-start
  41.5 0.1 fusion.46
  41.6 0.2 convert_reduce_fusion
  41.8 0.1 and_bitcast_fusion
  41.9 0.1 broadcast_in_dim.34
  42.0 0.1 pad.9.clone
  42.1 0.8 constant_dynamic-update-slice_fusion.1
  42.9 0.8 constant_dynamic-update-slice_fusion
  43.7 196.8 %all-to-all-done.1 = bf16[16,768,256]{1,2,0:T(8,128)(2,1)} async-done(((bf16[16,768,256]{1,2,0:T(8,128)(2,1)}), bf16[16,768,256]{1,2,0:T(8,128)(2,1)}, u32[]{:S(2)}, u32[]{:S(2)}) %all-to-all-start.1) | async-done | bytes 6291488 | tf_op jit(solution)/shard_map/all_to_all | solution.py:13
  240.5 4.7 convolution_convert_fusion.4
  245.2 5.0 all-gather.3.cloned.1.call-done
  250.2 9.1 %gather_fusion = bf16[12,256,896]{2,1,0:T(8,128)(2,1)} fusion(bf16[32,256,896]{2,1,0:T(8,128)(2,1)} %all-gather.3.cloned.1.call-done, s32[1024]{0:T(1024)S(1)} %pad_clamp_fusion), kind=kCustom, calls=%fused_computation | custom fusion | bytes 11010096 | tf_op jit(solution)/shard_map/jit(_take)/gather | solution.py:102
  259.3 3.8 bitcast_select_fusion
  263.0 4.8 convolution_convert_fusion.2
  267.9 1.6 copy-done.6
  269.5 0.7 slice.57
  270.2 2.8 collective-permute-start
  273.0 32.9 %all-gather.5.cloned.1.call-done = bf16[768,4096]{1,0:T(8,128)(2,1)} async-done(((bf16[768,256]{1,0:T(8,128)(2,1)}), bf16[768,4096]{1,0:T(8,128)(2,1)}) %all-gather.5.cloned.1.call-update) | async-done | bytes 6291472 | tf_op jit(solution)/shard_map/all_gather | solution.py:90
  305.9 5.2 convolution_convert_fusion.5
  311.1 0.4 maximum_maximum_fusion.1
  311.5 0.1 reshape.96
  311.6 0.1 reshape.101
  311.7 4.7 copy.52
  316.4 1.1 copy.51
  317.5 2.2 pad_maximum_fusion
  319.7 0.4 fusion.40
  320.1 0.8 copy-done.4
  320.9 1.8 exponential_reduce_fusion
  322.6 1.6 fusion.37
  324.2 6.4 %fusion.31 = f32[13,2,128,256]{3,2,1,0:T(8,128)} fusion(bf16[13,64,2,128]{3,2,1,0:T(2,128)(2,1)S(1)} %reshape.101, f32[13,2,64]{2,1,0:T(2,128)S(1)} %get-tuple-element.21, f32[13,2,64,256]{3,2,1,0:T(8,128)} %copy-done.3), kind=kOutput, calls=%fused_computation.48 | convolution fusion | flops 110757760 | bytes 5544448 | tf_op jit(solution)/shard_map/shqr,sqhe->srhe/dot_general | solution.py:49
  330.7 14.3 %fusion.11 = f32[13,2,128,256]{3,2,1,0:T(8,128)} fusion(f32[13,2,64,256]{3,2,1,0:T(8,128)} %fusion.37, bf16[13,64,2,128]{3,2,1,0:T(2,128)(2,1)S(1)} %reshape.96, f32[13,2,64,256]{3,2,1,0:T(8,128)} %get-tuple-element.22, f32[13,2,64]{2,1,0:T(2,128)S(1)} %get-tuple-element.21), kind=kOutput, calls=%fused_computation.27 | convolution fusion | flops 112035712 | bytes 7248384 | tf_op jit(solution)/shard_map/shqr,sqhe->srhe/dot_general | solution.py:46
  345.0 4.7 copy.64
  349.7 4.7 copy.65
  354.4 1.2 fusion.42
  355.6 5.1 collective-permute-start.1
  360.8 0.4 fusion.2
  361.2 5.3 collective-permute-done.1
  366.5 0.1 fusion.29
  366.6 6.0 %convert_bitcast_fusion = bf16[256,12,896]{0,2,1:T(8,128)(2,1)} fusion(bf16[12,256,512]{2,1,0:T(8,128)(2,1)S(1)} %fusion.29, bf16[896,512]{1,0:T(8,128)(2,1)} %constant_dynamic-update-slice_fusion), kind=kOutput, calls=%fused_computation.12 | convolution fusion | flops 2821324800 | bytes 9568256 | tf_op jit(solution)/shard_map/crk,dk->rcd/dot_general | solution.py:141
  372.6 11.4 %copy.66 = bf16[256,12,896]{2,1,0:T(8,128)(2,1)} copy(bf16[256,12,896]{0,2,1:T(8,128)(2,1)} %convert_bitcast_fusion) | data formatting | bytes 11010048 | tf_op jit(solution)/shard_map/convert_element_type | solution.py:143
  384.0 0.0 reduce-scatter.4.cloned.1.call-start
  384.1 4.9 fusion.22
  389.0 0.5 copy.56
  389.5 0.1 copy.85
  389.5 4.5 convolution_convert_fusion.1
  394.1 0.0 reduce-scatter.6.cloned.1.call-start
  394.1 12.9 %fusion.19 = bf16[13,64,2,128]{3,1,2,0:T(8,128)(2,1)S(1)} fusion(bf16[13,256,2,128]{1,3,2,0:T(8,128)(2,1)} %bitcast.65, f32[13,2,64,256]{3,2,1,0:T(8,128)} %fusion.37, f32[13,2,64,256]{3,2,1,0:T(8,128)} %get-tuple-element.22, f32[13,2,64]{2,1,0:T(2,128)S(1)} %get-tuple-element.21), kind=kOutput, calls=%fused_computation.33 | convolution fusion | flops 112248704 | bytes 5544448 | tf_op jit(solution)/shard_map/shqr,srhe->sqhe/dot_general | solution.py:43
  407.0 0.5 copy.61
  407.4 0.1 copy.84
  407.5 6.1 %convolution_convert_fusion = bf16[768,4096]{1,0:T(8,128)(2,1)} fusion(bf16[4096,256]{1,0:T(8,128)(2,1)} %param.13, bf16[832,256]{1,0:T(8,128)(2,1)S(1)} %bitcast.72), kind=kOutput, calls=%fused_computation.8 | convolution fusion | flops 1613758464 | bytes 8781824 | tf_op jit(solution)/shard_map/dot_general | solution.py:133
  413.6 39.1 %reduce-scatter.8.cloned.1.call-done = bf16[16,12,896]{2,1,0:T(8,128)(2,1)} async-done(((bf16[256,12,896]{2,1,0:T(8,128)(2,1)}), bf16[16,12,896]{2,1,0:T(8,128)(2,1)}) %reduce-scatter.8.cloned.1.call-update) | async-done | bytes 344080 | tf_op jit(solution)/shard_map/reduce_scatter | solution.py:140
  452.7 1.1 copy.67
  453.8 0.1 broadcast_in_dim.41
  453.9 1.0 scatter_fusion
  454.9 17.7 %all_to_all.16 = bf16[32,16,896]{2,1,0:T(8,128)(2,1)} all-to-all(bf16[32,16,896]{2,1,0:T(8,128)(2,1)S(1)} %scatter_fusion), channel_id=1, replica_groups=mesh['seq'=16,'mp'=16] {'seq'}, dimensions={0} | all-to-all | bytes 1835008 | tf_op jit(solution)/shard_map/all_to_all | solution.py:151
  472.6 48.5 %reduce-scatter.4.cloned.1.call-done = bf16[768,256]{1,0:T(8,128)(2,1)} async-done(((bf16[768,4096]{1,0:T(8,128)(2,1)}), bf16[768,256]{1,0:T(8,128)(2,1)}) %reduce-scatter.4.cloned.1.call-update) | async-done | bytes 393232 | tf_op jit(solution)/shard_map/reduce_scatter | solution.py:130
  521.1 67.9 %reduce-scatter.6.cloned.1.call-done = bf16[768,256]{1,0:T(8,128)(2,1)} async-done(((bf16[768,4096]{1,0:T(8,128)(2,1)}), bf16[768,256]{1,0:T(8,128)(2,1)}) %reduce-scatter.6.cloned.1.call-update) | async-done | bytes 393232 | tf_op jit(solution)/shard_map/reduce_scatter | solution.py:136
  589.1 2.2 copy.90
  (30 shorter events, 0.2 us)
Async XLA Ops:
  7.2 233.4 %copy-start = (bf16[256,4096]{1,0:T(8,128)(2,1)S(1)}, bf16[256,4096]{1,0:T(8,128)(2,1)}, u32[]{:S(2)}) copy-start(bf16[256,4096]{1,0:T(8,128)(2,1)} %param.16) | copy-start | bytes 6291460
  7.2 21.4 %copy-start.9 = (bf16[768,256]{1,0:T(8,128)(2,1)S(1)}, bf16[768,256]{1,0:T(8,128)(2,1)}, u32[]{:S(2)}) copy-start(bf16[768,256]{1,0:T(8,128)(2,1)} %param.17) | copy-start | bytes 1179652
  7.2 243.0 %all-gather.3.cloned.1.call-start = ((), (), s32[]{:S(2)}) async-start(), calls=%async_computation.6 | async-start | bytes 15597568 | tf_op jit(solution)/shard_map/all_gather | solution.py:101
  32.0 9.6 %copy-start.10 = (s32[192,1]{0,1:T(1,128)S(1)}, s32[192,1]{0,1:T(1,128)}, u32[]{:S(2)}) copy-start(s32[192,1]{0,1:T(1,128)} %param.12) | copy-start | bytes 2308
  32.0 10.1 %copy-start.7 = (bf16[896,256]{1,0:T(8,128)(2,1)S(1)}, bf16[896,256]{1,0:T(8,128)(2,1)}, u32[]{:S(2)}) copy-start(bf16[896,256]{1,0:T(8,128)(2,1)} %param.14) | copy-start | bytes 1376260
  32.0 10.9 %copy-start.8 = (bf16[896,256]{1,0:T(8,128)(2,1)S(1)}, bf16[896,256]{1,0:T(8,128)(2,1)}, u32[]{:S(2)}) copy-start(bf16[896,256]{1,0:T(8,128)(2,1)} %param.15) | copy-start | bytes 1376260
  32.0 208.5 %all-to-all-start.1 = ((bf16[16,768,256]{1,2,0:T(8,128)(2,1)}), bf16[16,768,256]{1,2,0:T(8,128)(2,1)}, u32[]{:S(2)}, u32[]{:S(2)}) async-start(bf16[16,768,256]{1,2,0:T(8,128)(2,1)} %stack.2), calls=%async_computation.2 | async-start | bytes 12582912 | tf_op jit(solution)/shard_map/all_to_all | solution.py:13
  40.7 265.2 %all-gather.5.cloned.1.call-start = ((), (), s32[]{:S(2)}) async-start(), calls=%async_computation.7 | async-start | bytes 6684672 | tf_op jit(solution)/shard_map/all_gather | solution.py:90
  41.5 411.3 %reduce-scatter.8.cloned.1.call-start = ((), (), s32[]{:S(2)}) async-start(), calls=%async_computation.10 | async-start | bytes 7798784 | tf_op jit(solution)/shard_map/reduce_scatter | solution.py:140
  267.9 1.7 copy-start.6
  270.2 46.1 %collective-permute-start = (bf16[256,512]{1,0:T(8,128)(2,1)}, bf16[256,512]{1,0:T(8,128)(2,1)}, u32[]{:S(2)}, u32[]{:S(2)}) collective-permute-start(bf16[256,512]{1,0:T(8,128)(2,1)} %slice.57), channel_id=1, source_target_pairs={{0,16},{16,32},{32,48},{48,64},{64,80},{80,96},{96,112},{112,128},... | collective-permute-start | bytes 786440 | tf_op jit(solution)/shard_map/ppermute | solution.py:20
  319.7 1.2 copy-start.4
  319.7 2.9 copy-start.5
  320.9 1.8 copy-start.3
  354.4 6.4 %copy-start.1 = (f32[13,256,256]{2,1,0:T(8,128)S(1)}, f32[13,256,256]{2,1,0:T(8,128)}, u32[]{:S(2)}) copy-start(f32[13,256,256]{2,1,0:T(8,128)} %copy.64) | copy-start | bytes 10223620
  354.4 6.4 %copy-start.2 = (f32[13,256,256]{2,1,0:T(8,128)S(1)}, f32[13,256,256]{2,1,0:T(8,128)}, u32[]{:S(2)}) copy-start(f32[13,256,256]{2,1,0:T(8,128)} %copy.65) | copy-start | bytes 10223620
  355.6 10.9 %collective-permute-start.1 = (bf16[256,512]{1,0:T(8,128)(2,1)S(1)}, bf16[256,512]{1,0:T(8,128)(2,1)S(1)}, u32[]{:S(2)}, u32[]{:S(2)}) collective-permute-start(bf16[256,512]{1,0:T(8,128)(2,1)S(1)} %fusion.42), channel_id=1, source_target_pairs={{16,0},{32,16},{48,32},{64,48},{80,64},{96,80},{112,96},{128,112},... | collective-permute-start | bytes 786440 | tf_op jit(solution)/shard_map/ppermute | solution.py:20
  384.0 137.1 %reduce-scatter.4.cloned.1.call-start = ((), (), s32[]{:S(2)}) async-start(), calls=%async_computation.8 | async-start | bytes 6684672 | tf_op jit(solution)/shard_map/reduce_scatter | solution.py:130
  394.1 195.0 %reduce-scatter.6.cloned.1.call-start = ((), (), s32[]{:S(2)}) async-start(), calls=%async_computation.9 | async-start | bytes 6684672 | tf_op jit(solution)/shard_map/reduce_scatter | solution.py:136
Sparse Core Ops, SparseCore 0:
  28.7 221.4 all-gather.2
  251.9 53.9 all-gather.4
  384.1 68.5 reduce-scatter.7
  455.7 65.3 reduce-scatter.3
  524.1 64.8 reduce-scatter.5
